TPU v7x, 32 devices: a whole 2x2x4 slice. The times are simulated.
32 devices in a mesh: groups: 2 (over x), path: 8 (over z, y), cons: 2 (over core).
Axes of the slice: x: 2, y: 2, z: 4, core: 2. Of those that a mesh axis runs over, the one named last changes fastest.
Arguments:
- tile_values: bfloat16 [16, 2, 32, 128, 128], P(('groups', 'path'), 'cons'), parts along dimension 0, may hold values from -0.125 to 0.125
- row_blocks: int32 [16, 2, 32], P(('groups', 'path'), 'cons'), parts along dimension 0, may hold values from 0 to 15, as said below
- col_blocks: int32 [16, 2, 32], P(('groups', 'path'), 'cons'), parts along dimension 0, may hold values from 0 to 7
- path_cost: float32 [16384], P(('groups', 'path', 'cons')), parts along dimension 0, may hold values from -6 to 6
- path_bound: float32 [16384], P(('groups', 'path', 'cons')), parts along dimension 0, may hold values from 0.5 to 2
- primal_start: float32 [16384], P(('groups', 'path', 'cons')), parts along dimension 0, may hold values from 0 to 1
- dual_start: float32 [8192], P(('groups', 'path', 'cons')), parts along dimension 0, may hold values from 0 to 1
- row_limits: float32 [8192], P(('groups', 'path', 'cons')), parts along dimension 0, may hold values from -6 to 6
- step_size: float32 [2], P('groups'), parts along dimension 0, may hold values from 0.3 to 0.45
- weight_start: float32 [2], P('groups'), parts along dimension 0, may hold values from 0.5 to 2
- restart_flags: int32 [12], P('groups'), parts along dimension 0, may hold values from 0 to 1
Outputs:
- primal_out: float32 [16384], P(('groups', 'path', 'cons')), parts along dimension 0
- dual_out: float32 [8192], P(('groups', 'path', 'cons')), parts along dimension 0
- link_loads: float32 [8192], P(('groups', 'path', 'cons')), parts along dimension 0
There are 2 independent parts, one for each index of `groups`. A program takes and returns all parts, laid end to end along the dimension named above; each array names one. Nothing has to cross between parts.
Inputs may be any that keep to these rules, and one draw needn't show every extreme that they name: `row_blocks`: row block of a tile inside its constraint half; for every device and every index o of path, at most 8 of the device's tiles lie in row blocks 2 * o to 2 * o + 1, and on every device some index o has exactly 8.
All inputs are finite; a program needn't handle non-finite values.
Results may differ from a plain program's by a relative error of at most 0.0031.
Values may be sent and summed in bfloat16 or wider, within the bound.
A program may use at most 64 MiB of HBM per device.

v0:
```python
import jax
import jax.numpy as jnp
from jax import lax
from jax.sharding import PartitionSpec as P


def tile_rows(tile_values, col_blocks, primal_low):
    blocks = primal_low.reshape(-1, tile_values.shape[-1])
    picked = blocks[col_blocks]
    return jnp.einsum("tij,tj->ti", tile_values, picked, preferred_element_type=jnp.float32)


def col_partial(tile_values, picked, col_blocks, col_count):
    products = jnp.einsum("tij,ti->tj", tile_values, picked, preferred_element_type=jnp.float32)
    return jax.ops.segment_sum(products, col_blocks, num_segments=col_count).reshape(-1)


def shards(
    tile_values,
    row_blocks,
    col_blocks,
    path_cost,
    path_bound,
    primal_start,
    dual_start,
    row_limits,
    step_size,
    weight_start,
    restart_flags,
):
    epsilon = 1e-06
    tile_values = tile_values[0, 0]
    row_blocks = row_blocks[0, 0]
    col_blocks = col_blocks[0, 0]
    edge = tile_values.shape[-1]
    primal_width = path_cost.shape[0]
    dual_width = row_limits.shape[0]
    col_count = primal_width * lax.axis_size("cons") // edge
    own_blocks = dual_width // edge
    path_count = lax.axis_size("path")
    tile_count = row_blocks.shape[0]
    capacity = max(2, (2 * tile_count + path_count - 1) // path_count)
    primal_now = primal_start
    dual_now = dual_start
    owners = row_blocks // own_blocks
    positions = jnp.arange(tile_count, dtype=jnp.int32)
    earlier = (owners[:, None] == owners[None, :]) & (positions[None, :] < positions[:, None])
    ranks = jnp.sum(earlier.astype(jnp.int32), axis=1)
    targets = owners * capacity + ranks
    slot_rows = (
        jnp.full((path_count * capacity,), -1, jnp.int32).at[targets].set(row_blocks % own_blocks)
    )
    arrived = lax.all_to_all(slot_rows, "path", split_axis=0, concat_axis=0, tiled=True)
    selector = (arrived[None, :] == jnp.arange(own_blocks, dtype=jnp.int32)[:, None]).astype(
        jnp.float32
    )
    reply_rows = jnp.maximum(arrived, 0)

    def primal_product(primal_low):
        primal_low = lax.all_gather(primal_low, "cons", axis=0, tiled=True)
        products = tile_rows(tile_values, col_blocks, primal_low)
        outgoing = jnp.zeros((path_count * capacity, edge), jnp.float32).at[targets].set(products)
        incoming = lax.all_to_all(outgoing, "path", split_axis=0, concat_axis=0, tiled=True)
        return jnp.dot(selector, incoming, precision=lax.Precision.HIGHEST).reshape(-1)

    anchor_primal = primal_now
    anchor_dual = dual_now
    primal_sum = jnp.zeros_like(primal_now)
    dual_sum = jnp.zeros_like(dual_now)
    steps_taken = jnp.zeros((), jnp.float32)
    eta = step_size[0]
    weight = weight_start[0]
    for turn_index in range(restart_flags.shape[0]):
        dual_low = dual_now.astype(jnp.bfloat16)
        replies = dual_low.reshape(own_blocks, edge)[reply_rows]
        returned = lax.all_to_all(replies, "path", split_axis=0, concat_axis=0, tiled=True)
        picked = returned[targets]
        partial_terms = col_partial(tile_values, picked, col_blocks, col_count)
        gradient = lax.psum_scatter(partial_terms, "cons", scatter_dimension=0, tiled=True)
        primal_next = jnp.clip(primal_now - eta / weight * (path_cost + gradient), 0.0, path_bound)
        extrapolated = (2.0 * primal_next - primal_now).astype(jnp.bfloat16)
        activity = primal_product(extrapolated)
        dual_next = jnp.maximum(dual_now + eta * weight * (activity - row_limits), 0.0)
        primal_sum = primal_sum + primal_next
        dual_sum = dual_sum + dual_next
        steps_taken = steps_taken + 1.0
        primal_mean = primal_sum / steps_taken
        dual_mean = dual_sum / steps_taken
        primal_shift = primal_mean - anchor_primal
        dual_shift = dual_mean - anchor_dual
        primal_move, dual_move = lax.psum(
            (jnp.sum(primal_shift * primal_shift), jnp.sum(dual_shift * dual_shift)),
            ("path", "cons"),
        )
        candidate = jnp.sqrt(
            weight * jnp.sqrt(dual_move + epsilon) / jnp.sqrt(primal_move + epsilon)
        )
        restart = restart_flags[turn_index] == 1
        primal_now = jnp.where(restart, primal_mean, primal_next)
        dual_now = jnp.where(restart, dual_mean, dual_next)
        anchor_primal = jnp.where(restart, primal_mean, anchor_primal)
        anchor_dual = jnp.where(restart, dual_mean, anchor_dual)
        primal_sum = jnp.where(restart, jnp.zeros_like(primal_sum), primal_sum)
        dual_sum = jnp.where(restart, jnp.zeros_like(dual_sum), dual_sum)
        steps_taken = jnp.where(restart, jnp.zeros((), jnp.float32), steps_taken)
        weight = jnp.where(restart, candidate, weight)
    loads = primal_product(primal_now.astype(jnp.bfloat16))
    return (primal_now, dual_now, loads)


def solution(mesh):
    in_specs = (
        P(("groups", "path"), "cons", None, None, None),
        P(("groups", "path"), "cons", None),
        P(("groups", "path"), "cons", None),
        P(("groups", "path", "cons")),
        P(("groups", "path", "cons")),
        P(("groups", "path", "cons")),
        P(("groups", "path", "cons")),
        P(("groups", "path", "cons")),
        P("groups"),
        P("groups"),
        P("groups"),
    )
    out_specs = (
        P(("groups", "path", "cons")),
        P(("groups", "path", "cons")),
        P(("groups", "path", "cons")),
    )
    return jax.shard_map(shards, mesh=mesh, in_specs=in_specs, out_specs=out_specs, check_vma=False)
```

profile of v0, /device:TPU:0, one launch (start us, length us, event | category | flops | bytes accessed | tf_op | source)
XLA Modules:
  0.0 356.9 jit_solution(11803322861526937581)
XLA Ops:
  0.6 0.8 and_select_fusion
  3.4 7.4 %all-to-all-start = ((s32[8,8,1]{1,2,0:T(1,128)}), s32[8,8,1]{1,2,0:T(1,128)S(1)}, u32[]{:S(2)}, u32[]{:S(2)}) async-start(s32[8,8,1]{1,2,0:T(1,128)} %bitcast.14), calls=%async_computation | async-start | bytes 8192 | tf_op jit(solution)/shard_map/all_to_all | solution.py:53
  11.5 5.8 %all-to-all-done = s32[8,8,1]{1,2,0:T(1,128)S(1)} async-done(((s32[8,8,1]{1,2,0:T(1,128)}), s32[8,8,1]{1,2,0:T(1,128)S(1)}, u32[]{:S(2)}, u32[]{:S(2)}) %all-to-all-start) | async-done | bytes 288 | tf_op jit(solution)/shard_map/all_to_all | solution.py:53
  18.6 1.2 gather_fusion
  19.8 3.3 all-to-all-start.1
  26.4 3.3 all-to-all-done.1
  30.6 0.7 scatter_custom_fusion.1
  31.4 2.5 all-reduce
  34.6 1.8 all-gather
  37.6 1.2 scatter_custom_fusion.2
  38.8 3.3 all-to-all-start.2
  42.3 6.5 %all-to-all-done.2 = f32[8,8,128]{2,1,0:T(8,128)S(1)} async-done(((f32[8,8,128]{2,1,0:T(8,128)}), f32[8,8,128]{2,1,0:T(8,128)S(1)}, u32[]{:S(2)}, u32[]{:S(2)}) %all-to-all-start.2) | async-done | bytes 32800 | tf_op jit(solution)/shard_map/all_to_all | solution.py:63
  49.6 1.2 gather_fusion.3
  50.8 3.5 all-to-all-start.3
  55.5 33.1 %all-reduce.10 = (f32[]{:T(128)}, f32[]{:T(128)}) all-reduce(f32[]{:T(128)} %get-tuple-element.40, f32[]{:T(128)} %get-tuple-element.33), channel_id=1, replica_groups=mesh['groups'=2,'path'=8,'cons'=2] {'path','cons'}, use_global_device_ids=true, to_apply=%region_6.7 | all-reduce | flops 2 | bytes 16 | tf_op jit(solution)/shard_map/psum | solution.py:91
  91.7 2.5 all-reduce.1
  94.9 1.8 all-gather.1
  98.0 1.2 scatter_custom_fusion.4
  99.2 3.3 all-to-all-start.4
  103.2 5.9 %all-to-all-done.4 = f32[8,8,128]{2,1,0:T(8,128)S(1)} async-done(((f32[8,8,128]{2,1,0:T(8,128)}), f32[8,8,128]{2,1,0:T(8,128)S(1)}, u32[]{:S(2)}, u32[]{:S(2)}) %all-to-all-start.4) | async-done | bytes 32800 | tf_op jit(solution)/shard_map/all_to_all | solution.py:63
  109.2 0.7 multiply_reduce_fusion.8
  109.9 1.2 gather_fusion.6
  111.1 3.3 all-to-all-start.5
  114.5 33.1 %all-reduce.9 = (f32[]{:T(128)}, f32[]{:T(128)}) all-reduce(f32[]{:T(128)} %get-tuple-element.31, f32[]{:T(128)} %get-tuple-element.29), channel_id=1, replica_groups=mesh['groups'=2,'path'=8,'cons'=2] {'path','cons'}, use_global_device_ids=true, to_apply=%region_13.14 | all-reduce | flops 2 | bytes 16 | tf_op jit(solution)/shard_map/psum | solution.py:91
  150.0 0.7 scatter_custom_fusion.5
  150.7 2.5 all-reduce.2
  153.2 0.8 multiply_reduce_fusion.2
  153.9 1.8 all-gather.2
  157.0 1.2 scatter_custom_fusion.6
  158.2 3.3 all-to-all-start.6
  162.2 6.0 %all-to-all-done.6 = f32[8,8,128]{2,1,0:T(8,128)S(1)} async-done(((f32[8,8,128]{2,1,0:T(8,128)}), f32[8,8,128]{2,1,0:T(8,128)S(1)}, u32[]{:S(2)}, u32[]{:S(2)}) %all-to-all-start.6) | async-done | bytes 32800 | tf_op jit(solution)/shard_map/all_to_all | solution.py:63
  168.2 0.7 multiply_reduce_fusion.7
  168.9 1.2 gather_fusion.9
  170.2 3.3 all-to-all-start.7
  173.5 33.1 %all-reduce.8 = (f32[]{:T(128)}, f32[]{:T(128)}) all-reduce(f32[]{:T(128)} %get-tuple-element.25, f32[]{:T(128)} %get-tuple-element.21), channel_id=1, replica_groups=mesh['groups'=2,'path'=8,'cons'=2] {'path','cons'}, use_global_device_ids=true, to_apply=%region_20.21 | all-reduce | flops 2 | bytes 16 | tf_op jit(solution)/shard_map/psum | solution.py:91
  209.0 0.7 scatter_custom_fusion.7
  209.7 2.5 all-reduce.3
  212.9 1.8 all-gather.3
  216.0 1.2 scatter_custom_fusion.8
  217.2 3.3 all-to-all-start.8
  221.2 6.0 %all-to-all-done.8 = f32[8,8,128]{2,1,0:T(8,128)S(1)} async-done(((f32[8,8,128]{2,1,0:T(8,128)}), f32[8,8,128]{2,1,0:T(8,128)S(1)}, u32[]{:S(2)}, u32[]{:S(2)}) %all-to-all-start.8) | async-done | bytes 32800 | tf_op jit(solution)/shard_map/all_to_all | solution.py:63
  227.2 0.7 multiply_reduce_fusion.6
  227.9 1.2 gather_fusion.12
  229.1 3.3 all-to-all-start.9
  232.5 33.1 %all-reduce.7 = (f32[]{:T(128)}, f32[]{:T(128)}) all-reduce(f32[]{:T(128)} %get-tuple-element.19, f32[]{:T(128)} %get-tuple-element.17), channel_id=1, replica_groups=mesh['groups'=2,'path'=8,'cons'=2] {'path','cons'}, use_global_device_ids=true, to_apply=%region_27.28 | all-reduce | flops 2 | bytes 16 | tf_op jit(solution)/shard_map/psum | solution.py:91
  268.1 0.7 scatter_custom_fusion.9
  268.8 2.5 all-reduce.4
  272.0 1.8 all-gather.4
  275.0 1.2 scatter_custom_fusion.10
  276.3 3.3 all-to-all-start.10
  280.2 6.0 %all-to-all-done.10 = f32[8,8,128]{2,1,0:T(8,128)S(1)} async-done(((f32[8,8,128]{2,1,0:T(8,128)}), f32[8,8,128]{2,1,0:T(8,128)S(1)}, u32[]{:S(2)}, u32[]{:S(2)}) %all-to-all-start.10) | async-done | bytes 32800 | tf_op jit(solution)/shard_map/all_to_all | solution.py:63
  287.0 1.2 gather_fusion.15
  288.2 3.3 all-to-all-start.11
  292.2 33.2 %all-reduce.6 = (f32[]{:T(128)}, f32[]{:T(128)}) all-reduce(f32[]{:T(128)} %get-tuple-element.38, f32[]{:T(128)} %get-tuple-element.36), channel_id=1, replica_groups=mesh['groups'=2,'path'=8,'cons'=2] {'path','cons'}, use_global_device_ids=true, to_apply=%region_34.35 | all-reduce | flops 2 | bytes 16 | tf_op jit(solution)/shard_map/psum | solution.py:91
  327.8 0.7 scatter_custom_fusion.11
  328.5 2.5 all-reduce.5
  331.7 1.8 all-gather.6
  334.7 1.2 scatter_custom_fusion.13
  336.0 3.3 all-to-all-start.13
  339.3 1.8 all-gather.5
  342.4 1.2 scatter_custom_fusion.12
  343.6 2.3 all-to-all-done.13
  345.9 3.6 %all-to-all-start.12 = ((f32[8,8,128]{2,1,0:T(8,128)}), f32[8,8,128]{2,1,0:T(8,128)S(1)}, u32[]{:S(2)}, u32[]{:S(2)}) async-start(f32[8,8,128]{2,1,0:T(8,128)} %bitcast.92), calls=%async_computation.12 | async-start | bytes 65536 | tf_op jit(solution)/shard_map/all_to_all | solution.py:63
  350.2 6.0 %all-to-all-done.12 = f32[8,8,128]{2,1,0:T(8,128)S(1)} async-done(((f32[8,8,128]{2,1,0:T(8,128)}), f32[8,8,128]{2,1,0:T(8,128)S(1)}, u32[]{:S(2)}, u32[]{:S(2)}) %all-to-all-start.12) | async-done | bytes 32800 | tf_op jit(solution)/shard_map/all_to_all | solution.py:63
  (106 shorter events, 27.8 us)
Async XLA Ops:
  0.6 29.6 %copy-start = (bf16[1,1,32,128,128]{4,3,2,1,0:T(8,128)(2,1)S(1)}, bf16[1,1,32,128,128]{4,3,2,1,0:T(8,128)(2,1)}, u32[]{:S(2)}) copy-start(bf16[1,1,32,128,128]{4,3,2,1,0:T(8,128)(2,1)} %param.11) | copy-start | bytes 3145732
  1.4 0.7 copy-start.7
  3.4 7.4 %copy-start.6 = (f32[256]{0:T(256)S(1)}, f32[256]{0:T(256)}, u32[]{:S(2)}) copy-start(f32[256]{0:T(256)} %param.17) | copy-start | bytes 3076
  3.4 13.9 %all-to-all-start = ((s32[8,8,1]{1,2,0:T(1,128)}), s32[8,8,1]{1,2,0:T(1,128)S(1)}, u32[]{:S(2)}, u32[]{:S(2)}) async-start(s32[8,8,1]{1,2,0:T(1,128)} %bitcast.14), calls=%async_computation | async-start | bytes 8192 | tf_op jit(solution)/shard_map/all_to_all | solution.py:53
  10.8 0.7 copy-start.8
  19.8 9.9 %all-to-all-start.1 = ((bf16[8,8,128]{2,1,0:T(8,128)(2,1)}), bf16[8,8,128]{2,1,0:T(8,128)(2,1)S(1)}, u32[]{:S(2)}, u32[]{:S(2)}) async-start(bf16[8,8,128]{2,1,0:T(8,128)(2,1)} %bitcast.15), calls=%async_computation.1 | async-start | bytes 32768 | tf_op jit(solution)/shard_map/all_to_all | solution.py:76
  24.5 0.7 copy-start.9
  31.4 2.5 copy-start.1
  31.4 2.5 copy-start.2
  31.4 2.5 copy-start.3
  38.8 10.0 %all-to-all-start.2 = ((f32[8,8,128]{2,1,0:T(8,128)}), f32[8,8,128]{2,1,0:T(8,128)S(1)}, u32[]{:S(2)}, u32[]{:S(2)}) async-start(f32[8,8,128]{2,1,0:T(8,128)} %bitcast.27), calls=%async_computation.2 | async-start | bytes 65536 | tf_op jit(solution)/shard_map/all_to_all | solution.py:63
  42.2 6.6 %copy-start.4 = (f32[256]{0:T(256)S(1)}, f32[256]{0:T(256)}, u32[]{:S(2)}) copy-start(f32[256]{0:T(256)} %param.18) | copy-start | bytes 3076
  50.8 3.5 copy-start.5
  50.8 39.3 %all-to-all-start.3 = ((bf16[8,8,128]{2,1,0:T(8,128)(2,1)}), bf16[8,8,128]{2,1,0:T(8,128)(2,1)S(1)}, u32[]{:S(2)}, u32[]{:S(2)}) async-start(bf16[8,8,128]{2,1,0:T(8,128)(2,1)} %bitcast.31), calls=%async_computation.3 | async-start | bytes 32768 | tf_op jit(solution)/shard_map/all_to_all | solution.py:76
  99.2 10.0 %all-to-all-start.4 = ((f32[8,8,128]{2,1,0:T(8,128)}), f32[8,8,128]{2,1,0:T(8,128)S(1)}, u32[]{:S(2)}, u32[]{:S(2)}) async-start(f32[8,8,128]{2,1,0:T(8,128)} %bitcast.40), calls=%async_computation.4 | async-start | bytes 65536 | tf_op jit(solution)/shard_map/all_to_all | solution.py:63
  111.1 37.9 %all-to-all-start.5 = ((bf16[8,8,128]{2,1,0:T(8,128)(2,1)}), bf16[8,8,128]{2,1,0:T(8,128)(2,1)S(1)}, u32[]{:S(2)}, u32[]{:S(2)}) async-start(bf16[8,8,128]{2,1,0:T(8,128)(2,1)} %bitcast.44), calls=%async_computation.5 | async-start | bytes 32768 | tf_op jit(solution)/shard_map/all_to_all | solution.py:76
  158.2 10.0 %all-to-all-start.6 = ((f32[8,8,128]{2,1,0:T(8,128)}), f32[8,8,128]{2,1,0:T(8,128)S(1)}, u32[]{:S(2)}, u32[]{:S(2)}) async-start(f32[8,8,128]{2,1,0:T(8,128)} %bitcast.53), calls=%async_computation.6 | async-start | bytes 65536 | tf_op jit(solution)/shard_map/all_to_all | solution.py:63
  170.2 37.9 %all-to-all-start.7 = ((bf16[8,8,128]{2,1,0:T(8,128)(2,1)}), bf16[8,8,128]{2,1,0:T(8,128)(2,1)S(1)}, u32[]{:S(2)}, u32[]{:S(2)}) async-start(bf16[8,8,128]{2,1,0:T(8,128)(2,1)} %bitcast.57), calls=%async_computation.7 | async-start | bytes 32768 | tf_op jit(solution)/shard_map/all_to_all | solution.py:76
  217.2 10.0 %all-to-all-start.8 = ((f32[8,8,128]{2,1,0:T(8,128)}), f32[8,8,128]{2,1,0:T(8,128)S(1)}, u32[]{:S(2)}, u32[]{:S(2)}) async-start(f32[8,8,128]{2,1,0:T(8,128)} %bitcast.66), calls=%async_computation.8 | async-start | bytes 65536 | tf_op jit(solution)/shard_map/all_to_all | solution.py:63
  229.1 38.0 %all-to-all-start.9 = ((bf16[8,8,128]{2,1,0:T(8,128)(2,1)}), bf16[8,8,128]{2,1,0:T(8,128)(2,1)S(1)}, u32[]{:S(2)}, u32[]{:S(2)}) async-start(bf16[8,8,128]{2,1,0:T(8,128)(2,1)} %bitcast.70), calls=%async_computation.9 | async-start | bytes 32768 | tf_op jit(solution)/shard_map/all_to_all | solution.py:76
  276.3 10.0 %all-to-all-start.10 = ((f32[8,8,128]{2,1,0:T(8,128)}), f32[8,8,128]{2,1,0:T(8,128)S(1)}, u32[]{:S(2)}, u32[]{:S(2)}) async-start(f32[8,8,128]{2,1,0:T(8,128)} %bitcast.79), calls=%async_computation.10 | async-start | bytes 65536 | tf_op jit(solution)/shard_map/all_to_all | solution.py:63
  288.2 38.6 %all-to-all-start.11 = ((bf16[8,8,128]{2,1,0:T(8,128)(2,1)}), bf16[8,8,128]{2,1,0:T(8,128)(2,1)S(1)}, u32[]{:S(2)}, u32[]{:S(2)}) async-start(bf16[8,8,128]{2,1,0:T(8,128)(2,1)} %bitcast.83), calls=%async_computation.11 | async-start | bytes 32768 | tf_op jit(solution)/shard_map/all_to_all | solution.py:76
  336.0 10.0 %all-to-all-start.13 = ((f32[8,8,128]{2,1,0:T(8,128)}), f32[8,8,128]{2,1,0:T(8,128)S(1)}, u32[]{:S(2)}, u32[]{:S(2)}) async-start(f32[8,8,128]{2,1,0:T(8,128)} %bitcast.98), calls=%async_computation.13 | async-start | bytes 65536 | tf_op jit(solution)/shard_map/all_to_all | solution.py:63
  345.9 10.3 %all-to-all-start.12 = ((f32[8,8,128]{2,1,0:T(8,128)}), f32[8,8,128]{2,1,0:T(8,128)S(1)}, u32[]{:S(2)}, u32[]{:S(2)}) async-start(f32[8,8,128]{2,1,0:T(8,128)} %bitcast.92), calls=%async_computation.12 | async-start | bytes 65536 | tf_op jit(solution)/shard_map/all_to_all | solution.py:63
where the time goes:
time: 358 us; the launch traced here: 357 us
  blocking collectives  193 us (54%)
  starting transfers between devices  51.1 us (14%)
  waiting for transfers between devices  47.8 us (13%)
  local copies, waits for them, and re-layouts  29 us (8%)
  between operations  14 us (4%)
  other arithmetic  11.6 us (3%)
  matrix products  10.6 us (3%)
    psum x5, blocking collectives, shards(): lax.psum((jnp.sum(primal_shift * primal_shift), jnp.sum(dual_shift * dual...  166 us
    all_to_all x7, waiting for transfers between devices, primal_product(): lax.all_to_all(outgoing, 'path', split_axis=0, concat_axis=0, tiled=True)  38.7 us
    all_to_all x7, starting transfers between devices, primal_product(): lax.all_to_all(outgoing, 'path', split_axis=0, concat_axis=0, tiled=True)  23.6 us
    all_to_all x6, starting transfers between devices, shards(): lax.all_to_all(replies, 'path', split_axis=0, concat_axis=0, tiled=True)  20.1 us
    unnamed x6, blocking collectives  14.8 us
    all_gather x7, blocking collectives, primal_product(): primal_low = lax.all_gather(primal_low, 'cons', axis=0, tiled=True)  12.4 us
    scatter x7, local copies, waits for them, and re-layouts, primal_product(): jnp.zeros((path_count * capacity, edge), jnp.float32).at[targets]  8.69 us
    all_to_all x1, starting transfers between devices, shards(): lax.all_to_all(slot_rows, 'path', split_axis=0, concat_axis=0, tiled=True)  7.41 us
  transfers between devices with their start and end apart: 14, of which 9 were waited for; matrix products, arithmetic and copies ran while one was open for 1% of the time, Pallas kernels for 0%

commit v1 on v0

--- a/solution.py
+++ b/solution.py
@@ -2,6 +2,32 @@
 import jax.numpy as jnp
 from jax import lax
 from jax.sharding import PartitionSpec as P
+
+
+def change_records(matrix, array_dim, target):
+    z1, outcome_arr = (matrix.shape[:array_dim], matrix.shape[array_dim + 1 :])
+    return jnp.moveaxis(matrix.reshape(*z1, target, -1, *outcome_arr), array_dim, 0)
+
+
+def _proceed_table(mine_x, dim_at):
+    mine_x = jnp.moveaxis(mine_x, 0, dim_at)
+    reached = mine_x.shape
+    return mine_x.reshape(
+        *reached[:dim_at], reached[dim_at] * reached[dim_at + 1], *reached[dim_at + 2 :]
+    )
+
+
+def press_packet_up(x0, along_axis, my_data, u=0):
+    block_out, x_now = (lax.axis_size(along_axis), lax.axis_index(along_axis))
+    frame_out = change_records(x0, my_data, block_out)
+    all_rows = [frame_out[x_now]]
+    for b in range(1, block_out):
+        extra = frame_out[x_now ^ b]
+        all_rows.append(
+            lax.ppermute(extra, along_axis, [(to_i, to_i ^ b) for to_i in range(block_out)])
+        )
+    frame_out = jnp.stack(all_rows)[x_now ^ jnp.arange(block_out)]
+    return _proceed_table(frame_out, u)
 
 
 def tile_rows(tile_values, col_blocks, primal_low):
@@ -73,7 +99,7 @@
     for turn_index in range(restart_flags.shape[0]):
         dual_low = dual_now.astype(jnp.bfloat16)
         replies = dual_low.reshape(own_blocks, edge)[reply_rows]
-        returned = lax.all_to_all(replies, "path", split_axis=0, concat_axis=0, tiled=True)
+        returned = press_packet_up(replies, "path", 0)
         picked = returned[targets]
         partial_terms = col_partial(tile_values, picked, col_blocks, col_count)
         gradient = lax.psum_scatter(partial_terms, "cons", scatter_dimension=0, tiled=True)

time: 358 us -> 409 us (1.14)
  starting transfers between devices: 51.1 us -> 94.8 us
  waiting for transfers between devices: 47.8 us -> 68.1 us
  blocking collectives: 193 us -> 178 us
    ppermute x0 -> x42, starting transfers between devices: none -> 53.4 us  [press_packet_up(): lax.ppermute(extra, along_axis, [(to_i, to_i ^ b) for to_i in range(block...]
    ppermute x0 -> x42, waiting for transfers between devices: none -> 23.9 us  [press_packet_up(): lax.ppermute(extra, along_axis, [(to_i, to_i ^ b) for to_i in range(block...]
    all_to_all x6 -> x0, starting transfers between devices: 20.1 us -> none  [shards(): lax.all_to_all(replies, 'path', split_axis=0, concat_axis=0, tiled=True)]
    psum x5, blocking collectives: 166 us -> 151 us  [shards(): lax.psum((jnp.sum(primal_shift * primal_shift), jnp.sum(dual_shift * dual...]
    all_to_all x7, starting transfers between devices: 23.6 us -> 34.1 us  [primal_product(): lax.all_to_all(outgoing, 'path', split_axis=0, concat_axis=0, tiled=True)]
  transfers between devices with their start and end apart: 14 -> 50, of which waited for: 9 -> 20; matrix products, arithmetic and copies ran while one was open for 1% -> 1% of each run, Pallas kernels for 0% -> 0%
where the time goes in v1:
time: 409 us; the launch traced here: 407 us
  blocking collectives  178 us (44%)
  starting transfers between devices  94.8 us (23%)
  waiting for transfers between devices  68.1 us (17%)
  local copies, waits for them, and re-layouts  30 us (7%)
  between operations  14.3 us (3%)
  other arithmetic  11.6 us (3%)
  matrix products  10.7 us (3%)
    psum x5, blocking collectives, shards(): lax.psum((jnp.sum(primal_shift * primal_shift), jnp.sum(dual_shift * dual...  151 us
    ppermute x42, starting transfers between devices, press_packet_up(): lax.ppermute(extra, along_axis, [(to_i, to_i ^ b) for to_i in range(block...  53.4 us
    all_to_all x7, waiting for transfers between devices, primal_product(): lax.all_to_all(outgoing, 'path', split_axis=0, concat_axis=0, tiled=True)  39.1 us
    all_to_all x7, starting transfers between devices, primal_product(): lax.all_to_all(outgoing, 'path', split_axis=0, concat_axis=0, tiled=True)  34.1 us
    ppermute x42, waiting for transfers between devices, press_packet_up(): lax.ppermute(extra, along_axis, [(to_i, to_i ^ b) for to_i in range(block...  23.9 us
    unnamed x6, blocking collectives  14.8 us
    all_gather x7, blocking collectives, primal_product(): primal_low = lax.all_gather(primal_low, 'cons', axis=0, tiled=True)  12.4 us
    scatter x7, local copies, waits for them, and re-layouts, primal_product(): jnp.zeros((path_count * capacity, edge), jnp.float32).at[targets]  8.69 us
  transfers between devices with their start and end apart: 50, of which 20 were waited for; matrix products, arithmetic and copies ran while one was open for 1% of the time, Pallas kernels for 0%

profile of v1, /device:TPU:0, one launch (start us, length us, event | category | flops | bytes accessed | tf_op | source)
XLA Modules:
  0.0 407.4 jit_solution(3274574257460727536)
XLA Ops:
  3.4 7.3 %all-to-all-start = ((s32[8,8,1]{1,2,0:T(1,128)}), s32[8,8,1]{1,2,0:T(1,128)S(1)}, u32[]{:S(2)}, u32[]{:S(2)}) async-start(s32[8,8,1]{1,2,0:T(1,128)} %bitcast.14), calls=%async_computation | async-start | bytes 8192 | tf_op jit(solution)/shard_map/all_to_all | solution.py:79
  12.0 5.1 %all-to-all-done = s32[8,8,1]{1,2,0:T(1,128)S(1)} async-done(((s32[8,8,1]{1,2,0:T(1,128)}), s32[8,8,1]{1,2,0:T(1,128)S(1)}, u32[]{:S(2)}, u32[]{:S(2)}) %all-to-all-start) | async-done | bytes 288 | tf_op jit(solution)/shard_map/all_to_all | solution.py:79
  23.6 2.4 collective-permute-start.2
  26.5 2.4 collective-permute-start.4
  29.5 4.2 %collective-permute-start.6 = (bf16[8,128]{1,0:T(8,128)(2,1)S(1)}, bf16[8,128]{1,0:T(8,128)(2,1)S(1)}, u32[]{:S(2)}, u32[]{:S(2)}) collective-permute-start(bf16[8,128]{1,0:T(8,128)(2,1)S(1)} %get-tuple-element.76), channel_id=1, source_target_pairs={{0,14},{2,12},{4,10},{6,8},{8,6},{10,4},{12,2},{14,0},{1,15},{3,13... | collective-permute-start | bytes 6152 | tf_op jit(solution)/shard_map/ppermute | solution.py:27
  34.3 1.5 collective-permute-done.6
  38.1 2.5 all-reduce
  41.2 1.8 all-gather
  44.3 1.2 scatter_custom_fusion.2
  45.5 5.4 %all-to-all-start.1 = ((f32[8,8,128]{2,1,0:T(8,128)}), f32[8,8,128]{2,1,0:T(8,128)S(1)}, u32[]{:S(2)}, u32[]{:S(2)}) async-start(f32[8,8,128]{2,1,0:T(8,128)} %bitcast.42), calls=%async_computation.1 | async-start | bytes 65536 | tf_op jit(solution)/shard_map/all_to_all | solution.py:89
  51.0 6.6 %all-to-all-done.1 = f32[8,8,128]{2,1,0:T(8,128)S(1)} async-done(((f32[8,8,128]{2,1,0:T(8,128)}), f32[8,8,128]{2,1,0:T(8,128)S(1)}, u32[]{:S(2)}, u32[]{:S(2)}) %all-to-all-start.1) | async-done | bytes 32800 | tf_op jit(solution)/shard_map/all_to_all | solution.py:89
  61.0 30.0 %all-reduce.10 = (f32[]{:T(128)}, f32[]{:T(128)}) all-reduce(f32[]{:T(128)} %get-tuple-element.88, f32[]{:T(128)} %get-tuple-element.33), channel_id=1, replica_groups=mesh['groups'=2,'path'=8,'cons'=2] {'path','cons'}, use_global_device_ids=true, to_apply=%region_6.7 | all-reduce | flops 2 | bytes 16 | tf_op jit(solution)/shard_map/psum | solution.py:117
  92.5 5.7 %collective-permute-start.11 = (bf16[8,128]{1,0:T(8,128)(2,1)S(1)}, bf16[8,128]{1,0:T(8,128)(2,1)S(1)}, u32[]{:S(2)}, u32[]{:S(2)}) collective-permute-start(bf16[8,128]{1,0:T(8,128)(2,1)S(1)} %get-tuple-element.70), channel_id=1, source_target_pairs={{0,10},{2,8},{4,14},{6,12},{8,2},{10,0},{12,6},{14,4},{1,11},{3,9}... | collective-permute-start | bytes 6152 | tf_op jit(solution)/shard_map/ppermute | solution.py:27
  98.4 1.9 collective-permute-start.13
  100.4 3.4 collective-permute-done.12
  103.7 1.0 collective-permute-done.13
  107.0 2.5 all-reduce.1
  110.2 1.8 all-gather.1
  113.2 1.2 scatter_custom_fusion.4
  114.5 5.0 %all-to-all-start.2 = ((f32[8,8,128]{2,1,0:T(8,128)}), f32[8,8,128]{2,1,0:T(8,128)S(1)}, u32[]{:S(2)}, u32[]{:S(2)}) async-start(f32[8,8,128]{2,1,0:T(8,128)} %bitcast.69), calls=%async_computation.2 | async-start | bytes 65536 | tf_op jit(solution)/shard_map/all_to_all | solution.py:89
  120.2 6.0 %all-to-all-done.2 = f32[8,8,128]{2,1,0:T(8,128)S(1)} async-done(((f32[8,8,128]{2,1,0:T(8,128)}), f32[8,8,128]{2,1,0:T(8,128)S(1)}, u32[]{:S(2)}, u32[]{:S(2)}) %all-to-all-start.2) | async-done | bytes 32800 | tf_op jit(solution)/shard_map/all_to_all | solution.py:89
  128.2 30.2 %all-reduce.9 = (f32[]{:T(128)}, f32[]{:T(128)}) all-reduce(f32[]{:T(128)} %get-tuple-element.31, f32[]{:T(128)} %get-tuple-element.29), channel_id=1, replica_groups=mesh['groups'=2,'path'=8,'cons'=2] {'path','cons'}, use_global_device_ids=true, to_apply=%region_13.14 | all-reduce | flops 2 | bytes 16 | tf_op jit(solution)/shard_map/psum | solution.py:117
  160.0 5.7 %collective-permute-start.18 = (bf16[8,128]{1,0:T(8,128)(2,1)S(1)}, bf16[8,128]{1,0:T(8,128)(2,1)S(1)}, u32[]{:S(2)}, u32[]{:S(2)}) collective-permute-start(bf16[8,128]{1,0:T(8,128)(2,1)S(1)} %get-tuple-element.62), channel_id=1, source_target_pairs={{0,10},{2,8},{4,14},{6,12},{8,2},{10,0},{12,6},{14,4},{1,11},{3,9}... | collective-permute-start | bytes 6152 | tf_op jit(solution)/shard_map/ppermute | solution.py:27
  165.8 1.9 collective-permute-start.20
  167.8 3.4 collective-permute-done.19
  171.2 1.0 collective-permute-done.20
  174.5 2.5 all-reduce.2
  177.7 1.8 all-gather.2
  180.8 1.2 scatter_custom_fusion.6
  182.0 5.0 %all-to-all-start.3 = ((f32[8,8,128]{2,1,0:T(8,128)}), f32[8,8,128]{2,1,0:T(8,128)S(1)}, u32[]{:S(2)}, u32[]{:S(2)}) async-start(f32[8,8,128]{2,1,0:T(8,128)} %bitcast.96), calls=%async_computation.3 | async-start | bytes 65536 | tf_op jit(solution)/shard_map/all_to_all | solution.py:89
  187.7 6.0 %all-to-all-done.3 = f32[8,8,128]{2,1,0:T(8,128)S(1)} async-done(((f32[8,8,128]{2,1,0:T(8,128)}), f32[8,8,128]{2,1,0:T(8,128)S(1)}, u32[]{:S(2)}, u32[]{:S(2)}) %all-to-all-start.3) | async-done | bytes 32800 | tf_op jit(solution)/shard_map/all_to_all | solution.py:89
  195.7 30.1 %all-reduce.8 = (f32[]{:T(128)}, f32[]{:T(128)}) all-reduce(f32[]{:T(128)} %get-tuple-element.25, f32[]{:T(128)} %get-tuple-element.21), channel_id=1, replica_groups=mesh['groups'=2,'path'=8,'cons'=2] {'path','cons'}, use_global_device_ids=true, to_apply=%region_20.21 | all-reduce | flops 2 | bytes 16 | tf_op jit(solution)/shard_map/psum | solution.py:117
  227.4 5.7 %collective-permute-start.25 = (bf16[8,128]{1,0:T(8,128)(2,1)S(1)}, bf16[8,128]{1,0:T(8,128)(2,1)S(1)}, u32[]{:S(2)}, u32[]{:S(2)}) collective-permute-start(bf16[8,128]{1,0:T(8,128)(2,1)S(1)} %get-tuple-element.54), channel_id=1, source_target_pairs={{0,10},{2,8},{4,14},{6,12},{8,2},{10,0},{12,6},{14,4},{1,11},{3,9}... | collective-permute-start | bytes 6152 | tf_op jit(solution)/shard_map/ppermute | solution.py:27
  233.3 1.9 collective-permute-start.27
  235.2 3.4 collective-permute-done.26
  238.6 1.0 collective-permute-done.27
  241.9 2.5 all-reduce.3
  245.1 1.8 all-gather.3
  248.1 1.2 scatter_custom_fusion.8
  249.3 5.0 %all-to-all-start.4 = ((f32[8,8,128]{2,1,0:T(8,128)}), f32[8,8,128]{2,1,0:T(8,128)S(1)}, u32[]{:S(2)}, u32[]{:S(2)}) async-start(f32[8,8,128]{2,1,0:T(8,128)} %bitcast.123), calls=%async_computation.4 | async-start | bytes 65536 | tf_op jit(solution)/shard_map/all_to_all | solution.py:89
  255.0 6.0 %all-to-all-done.4 = f32[8,8,128]{2,1,0:T(8,128)S(1)} async-done(((f32[8,8,128]{2,1,0:T(8,128)}), f32[8,8,128]{2,1,0:T(8,128)S(1)}, u32[]{:S(2)}, u32[]{:S(2)}) %all-to-all-start.4) | async-done | bytes 32800 | tf_op jit(solution)/shard_map/all_to_all | solution.py:89
  263.0 30.1 %all-reduce.7 = (f32[]{:T(128)}, f32[]{:T(128)}) all-reduce(f32[]{:T(128)} %get-tuple-element.19, f32[]{:T(128)} %get-tuple-element.17), channel_id=1, replica_groups=mesh['groups'=2,'path'=8,'cons'=2] {'path','cons'}, use_global_device_ids=true, to_apply=%region_27.28 | all-reduce | flops 2 | bytes 16 | tf_op jit(solution)/shard_map/psum | solution.py:117
  294.8 5.7 %collective-permute-start.32 = (bf16[8,128]{1,0:T(8,128)(2,1)S(1)}, bf16[8,128]{1,0:T(8,128)(2,1)S(1)}, u32[]{:S(2)}, u32[]{:S(2)}) collective-permute-start(bf16[8,128]{1,0:T(8,128)(2,1)S(1)} %get-tuple-element.46), channel_id=1, source_target_pairs={{0,10},{2,8},{4,14},{6,12},{8,2},{10,0},{12,6},{14,4},{1,11},{3,9}... | collective-permute-start | bytes 6152 | tf_op jit(solution)/shard_map/ppermute | solution.py:27
  300.6 1.9 collective-permute-start.34
  302.6 3.4 collective-permute-done.33
  306.0 1.0 collective-permute-done.34
  309.2 2.5 all-reduce.4
  312.4 1.8 all-gather.4
  315.4 1.2 scatter_custom_fusion.10
  316.7 5.0 %all-to-all-start.5 = ((f32[8,8,128]{2,1,0:T(8,128)}), f32[8,8,128]{2,1,0:T(8,128)S(1)}, u32[]{:S(2)}, u32[]{:S(2)}) async-start(f32[8,8,128]{2,1,0:T(8,128)} %bitcast.150), calls=%async_computation.5 | async-start | bytes 65536 | tf_op jit(solution)/shard_map/all_to_all | solution.py:89
  322.3 6.0 %all-to-all-done.5 = f32[8,8,128]{2,1,0:T(8,128)S(1)} async-done(((f32[8,8,128]{2,1,0:T(8,128)}), f32[8,8,128]{2,1,0:T(8,128)S(1)}, u32[]{:S(2)}, u32[]{:S(2)}) %all-to-all-start.5) | async-done | bytes 32800 | tf_op jit(solution)/shard_map/all_to_all | solution.py:89
  331.0 30.1 %all-reduce.6 = (f32[]{:T(128)}, f32[]{:T(128)}) all-reduce(f32[]{:T(128)} %get-tuple-element.86, f32[]{:T(128)} %get-tuple-element.84), channel_id=1, replica_groups=mesh['groups'=2,'path'=8,'cons'=2] {'path','cons'}, use_global_device_ids=true, to_apply=%region_34.35 | all-reduce | flops 2 | bytes 16 | tf_op jit(solution)/shard_map/psum | solution.py:117
  362.8 5.7 %collective-permute-start.39 = (bf16[8,128]{1,0:T(8,128)(2,1)S(1)}, bf16[8,128]{1,0:T(8,128)(2,1)S(1)}, u32[]{:S(2)}, u32[]{:S(2)}) collective-permute-start(bf16[8,128]{1,0:T(8,128)(2,1)S(1)} %get-tuple-element.38), channel_id=1, source_target_pairs={{0,10},{2,8},{4,14},{6,12},{8,2},{10,0},{12,6},{14,4},{1,11},{3,9}... | collective-permute-start | bytes 6152 | tf_op jit(solution)/shard_map/ppermute | solution.py:27
  368.6 1.9 collective-permute-start.41
  370.6 3.4 collective-permute-done.40
  377.2 2.5 all-reduce.5
  380.4 1.8 all-gather.6
  383.4 1.2 scatter_custom_fusion.13
  384.7 5.0 %all-to-all-start.7 = ((f32[8,8,128]{2,1,0:T(8,128)}), f32[8,8,128]{2,1,0:T(8,128)S(1)}, u32[]{:S(2)}, u32[]{:S(2)}) async-start(f32[8,8,128]{2,1,0:T(8,128)} %bitcast.183), calls=%async_computation.7 | async-start | bytes 65536 | tf_op jit(solution)/shard_map/all_to_all | solution.py:89
  389.7 1.8 all-gather.5
  392.7 1.2 scatter_custom_fusion.12
  394.0 2.4 all-to-all-done.7
  396.4 3.6 all-to-all-start.6
  400.7 6.0 %all-to-all-done.6 = f32[8,8,128]{2,1,0:T(8,128)S(1)} async-done(((f32[8,8,128]{2,1,0:T(8,128)}), f32[8,8,128]{2,1,0:T(8,128)S(1)}, u32[]{:S(2)}, u32[]{:S(2)}) %all-to-all-start.6) | async-done | bytes 32800 | tf_op jit(solution)/shard_map/all_to_all | solution.py:89
  (233 shorter events, 51.9 us)
Async XLA Ops:
  0.6 36.3 %copy-start = (bf16[1,1,32,128,128]{4,3,2,1,0:T(8,128)(2,1)S(1)}, bf16[1,1,32,128,128]{4,3,2,1,0:T(8,128)(2,1)}, u32[]{:S(2)}) copy-start(bf16[1,1,32,128,128]{4,3,2,1,0:T(8,128)(2,1)} %param.11) | copy-start | bytes 3145732
  1.4 0.7 copy-start.7
  3.4 13.7 %all-to-all-start = ((s32[8,8,1]{1,2,0:T(1,128)}), s32[8,8,1]{1,2,0:T(1,128)S(1)}, u32[]{:S(2)}, u32[]{:S(2)}) async-start(s32[8,8,1]{1,2,0:T(1,128)} %bitcast.14), calls=%async_computation | async-start | bytes 8192 | tf_op jit(solution)/shard_map/all_to_all | solution.py:79
  10.7 0.7 copy-start.6
  11.4 0.7 copy-start.8
  19.1 9.8 %collective-permute-start = (bf16[8,128]{1,0:T(8,128)(2,1)S(1)}, bf16[8,128]{1,0:T(8,128)(2,1)S(1)}, u32[]{:S(2)}, u32[]{:S(2)}) collective-permute-start(bf16[8,128]{1,0:T(8,128)(2,1)S(1)} %get-tuple-element.82), channel_id=1, source_target_pairs={{0,2},{2,0},{4,6},{6,4},{8,10},{10,8},{12,14},{14,12},{1,3},{3,1},... | collective-permute-start | bytes 6152 | tf_op jit(solution)/shard_map/ppermute | solution.py:27
  21.1 0.7 copy-start.9
  23.0 6.5 %collective-permute-start.1 = (bf16[8,128]{1,0:T(8,128)(2,1)S(1)}, bf16[8,128]{1,0:T(8,128)(2,1)S(1)}, u32[]{:S(2)}, u32[]{:S(2)}) collective-permute-start(bf16[8,128]{1,0:T(8,128)(2,1)S(1)} %get-tuple-element.81), channel_id=1, source_target_pairs={{0,4},{2,6},{4,0},{6,2},{8,12},{10,14},{12,8},{14,10},{1,5},{3,7},... | collective-permute-start | bytes 6152 | tf_op jit(solution)/shard_map/ppermute | solution.py:27
  23.6 10.0 %collective-permute-start.2 = (bf16[8,128]{1,0:T(8,128)(2,1)S(1)}, bf16[8,128]{1,0:T(8,128)(2,1)S(1)}, u32[]{:S(2)}, u32[]{:S(2)}) collective-permute-start(bf16[8,128]{1,0:T(8,128)(2,1)S(1)} %get-tuple-element.80), channel_id=1, source_target_pairs={{0,6},{2,4},{4,2},{6,0},{8,14},{10,12},{12,10},{14,8},{1,7},{3,5},... | collective-permute-start | bytes 6152 | tf_op jit(solution)/shard_map/ppermute | solution.py:27
  26.0 7.7 %collective-permute-start.3 = (bf16[8,128]{1,0:T(8,128)(2,1)S(1)}, bf16[8,128]{1,0:T(8,128)(2,1)S(1)}, u32[]{:S(2)}, u32[]{:S(2)}) collective-permute-start(bf16[8,128]{1,0:T(8,128)(2,1)S(1)} %get-tuple-element.79), channel_id=1, source_target_pairs={{0,8},{2,10},{4,12},{6,14},{8,0},{10,2},{12,4},{14,6},{1,9},{3,11}... | collective-permute-start | bytes 6152 | tf_op jit(solution)/shard_map/ppermute | solution.py:27
  26.5 7.1 %collective-permute-start.4 = (bf16[8,128]{1,0:T(8,128)(2,1)S(1)}, bf16[8,128]{1,0:T(8,128)(2,1)S(1)}, u32[]{:S(2)}, u32[]{:S(2)}) collective-permute-start(bf16[8,128]{1,0:T(8,128)(2,1)S(1)} %get-tuple-element.78), channel_id=1, source_target_pairs={{0,10},{2,8},{4,14},{6,12},{8,2},{10,0},{12,6},{14,4},{1,11},{3,9}... | collective-permute-start | bytes 6152 | tf_op jit(solution)/shard_map/ppermute | solution.py:27
  28.9 5.4 %collective-permute-start.5 = (bf16[8,128]{1,0:T(8,128)(2,1)S(1)}, bf16[8,128]{1,0:T(8,128)(2,1)S(1)}, u32[]{:S(2)}, u32[]{:S(2)}) collective-permute-start(bf16[8,128]{1,0:T(8,128)(2,1)S(1)} %get-tuple-element.77), channel_id=1, source_target_pairs={{0,12},{2,14},{4,8},{6,10},{8,4},{10,6},{12,0},{14,2},{1,13},{3,15... | collective-permute-start | bytes 6152 | tf_op jit(solution)/shard_map/ppermute | solution.py:27
  29.5 6.3 %collective-permute-start.6 = (bf16[8,128]{1,0:T(8,128)(2,1)S(1)}, bf16[8,128]{1,0:T(8,128)(2,1)S(1)}, u32[]{:S(2)}, u32[]{:S(2)}) collective-permute-start(bf16[8,128]{1,0:T(8,128)(2,1)S(1)} %get-tuple-element.76), channel_id=1, source_target_pairs={{0,14},{2,12},{4,10},{6,8},{8,6},{10,4},{12,2},{14,0},{1,15},{3,13... | collective-permute-start | bytes 6152 | tf_op jit(solution)/shard_map/ppermute | solution.py:27
  38.0 2.5 copy-start.1
  38.1 2.5 copy-start.2
  38.1 2.5 copy-start.3
  45.5 12.1 %all-to-all-start.1 = ((f32[8,8,128]{2,1,0:T(8,128)}), f32[8,8,128]{2,1,0:T(8,128)S(1)}, u32[]{:S(2)}, u32[]{:S(2)}) async-start(f32[8,8,128]{2,1,0:T(8,128)} %bitcast.42), calls=%async_computation.1 | async-start | bytes 65536 | tf_op jit(solution)/shard_map/all_to_all | solution.py:89
  51.0 6.7 %copy-start.4 = (f32[256]{0:T(256)S(1)}, f32[256]{0:T(256)}, u32[]{:S(2)}) copy-start(f32[256]{0:T(256)} %param.18) | copy-start | bytes 3076
  59.1 0.7 copy-start.5
  59.1 39.1 %collective-permute-start.7 = (bf16[8,128]{1,0:T(8,128)(2,1)S(1)}, bf16[8,128]{1,0:T(8,128)(2,1)S(1)}, u32[]{:S(2)}, u32[]{:S(2)}) collective-permute-start(bf16[8,128]{1,0:T(8,128)(2,1)S(1)} %get-tuple-element.74), channel_id=1, source_target_pairs={{0,2},{2,0},{4,6},{6,4},{8,10},{10,8},{12,14},{14,12},{1,3},{3,1},... | collective-permute-start | bytes 6152 | tf_op jit(solution)/shard_map/ppermute | solution.py:27
  92.3 6.1 %collective-permute-start.8 = (bf16[8,128]{1,0:T(8,128)(2,1)S(1)}, bf16[8,128]{1,0:T(8,128)(2,1)S(1)}, u32[]{:S(2)}, u32[]{:S(2)}) collective-permute-start(bf16[8,128]{1,0:T(8,128)(2,1)S(1)} %get-tuple-element.73), channel_id=1, source_target_pairs={{0,4},{2,6},{4,0},{6,2},{8,12},{10,14},{12,8},{14,10},{1,5},{3,7},... | collective-permute-start | bytes 6152 | tf_op jit(solution)/shard_map/ppermute | solution.py:27
  92.4 7.9 %collective-permute-start.9 = (bf16[8,128]{1,0:T(8,128)(2,1)S(1)}, bf16[8,128]{1,0:T(8,128)(2,1)S(1)}, u32[]{:S(2)}, u32[]{:S(2)}) collective-permute-start(bf16[8,128]{1,0:T(8,128)(2,1)S(1)} %get-tuple-element.72), channel_id=1, source_target_pairs={{0,6},{2,4},{4,2},{6,0},{8,14},{10,12},{12,10},{14,8},{1,7},{3,5},... | collective-permute-start | bytes 6152 | tf_op jit(solution)/shard_map/ppermute | solution.py:27
  92.5 7.9 %collective-permute-start.10 = (bf16[8,128]{1,0:T(8,128)(2,1)S(1)}, bf16[8,128]{1,0:T(8,128)(2,1)S(1)}, u32[]{:S(2)}, u32[]{:S(2)}) collective-permute-start(bf16[8,128]{1,0:T(8,128)(2,1)S(1)} %get-tuple-element.71), channel_id=1, source_target_pairs={{0,8},{2,10},{4,12},{6,14},{8,0},{10,2},{12,4},{14,6},{1,9},{3,11}... | collective-permute-start | bytes 6152 | tf_op jit(solution)/shard_map/ppermute | solution.py:27
  92.5 7.8 %collective-permute-start.11 = (bf16[8,128]{1,0:T(8,128)(2,1)S(1)}, bf16[8,128]{1,0:T(8,128)(2,1)S(1)}, u32[]{:S(2)}, u32[]{:S(2)}) collective-permute-start(bf16[8,128]{1,0:T(8,128)(2,1)S(1)} %get-tuple-element.70), channel_id=1, source_target_pairs={{0,10},{2,8},{4,14},{6,12},{8,2},{10,0},{12,6},{14,4},{1,11},{3,9}... | collective-permute-start | bytes 6152 | tf_op jit(solution)/shard_map/ppermute | solution.py:27
  98.3 5.4 %collective-permute-start.12 = (bf16[8,128]{1,0:T(8,128)(2,1)S(1)}, bf16[8,128]{1,0:T(8,128)(2,1)S(1)}, u32[]{:S(2)}, u32[]{:S(2)}) collective-permute-start(bf16[8,128]{1,0:T(8,128)(2,1)S(1)} %get-tuple-element.69), channel_id=1, source_target_pairs={{0,12},{2,14},{4,8},{6,10},{8,4},{10,6},{12,0},{14,2},{1,13},{3,15... | collective-permute-start | bytes 6152 | tf_op jit(solution)/shard_map/ppermute | solution.py:27
  98.4 6.3 %collective-permute-start.13 = (bf16[8,128]{1,0:T(8,128)(2,1)S(1)}, bf16[8,128]{1,0:T(8,128)(2,1)S(1)}, u32[]{:S(2)}, u32[]{:S(2)}) collective-permute-start(bf16[8,128]{1,0:T(8,128)(2,1)S(1)} %get-tuple-element.68), channel_id=1, source_target_pairs={{0,14},{2,12},{4,10},{6,8},{8,6},{10,4},{12,2},{14,0},{1,15},{3,13... | collective-permute-start | bytes 6152 | tf_op jit(solution)/shard_map/ppermute | solution.py:27
  114.5 11.7 %all-to-all-start.2 = ((f32[8,8,128]{2,1,0:T(8,128)}), f32[8,8,128]{2,1,0:T(8,128)S(1)}, u32[]{:S(2)}, u32[]{:S(2)}) async-start(f32[8,8,128]{2,1,0:T(8,128)} %bitcast.69), calls=%async_computation.2 | async-start | bytes 65536 | tf_op jit(solution)/shard_map/all_to_all | solution.py:89
  127.6 38.1 %collective-permute-start.14 = (bf16[8,128]{1,0:T(8,128)(2,1)S(1)}, bf16[8,128]{1,0:T(8,128)(2,1)S(1)}, u32[]{:S(2)}, u32[]{:S(2)}) collective-permute-start(bf16[8,128]{1,0:T(8,128)(2,1)S(1)} %get-tuple-element.66), channel_id=1, source_target_pairs={{0,2},{2,0},{4,6},{6,4},{8,10},{10,8},{12,14},{14,12},{1,3},{3,1},... | collective-permute-start | bytes 6152 | tf_op jit(solution)/shard_map/ppermute | solution.py:27
  159.8 6.1 %collective-permute-start.15 = (bf16[8,128]{1,0:T(8,128)(2,1)S(1)}, bf16[8,128]{1,0:T(8,128)(2,1)S(1)}, u32[]{:S(2)}, u32[]{:S(2)}) collective-permute-start(bf16[8,128]{1,0:T(8,128)(2,1)S(1)} %get-tuple-element.65), channel_id=1, source_target_pairs={{0,4},{2,6},{4,0},{6,2},{8,12},{10,14},{12,8},{14,10},{1,5},{3,7},... | collective-permute-start | bytes 6152 | tf_op jit(solution)/shard_map/ppermute | solution.py:27
  159.8 7.9 %collective-permute-start.16 = (bf16[8,128]{1,0:T(8,128)(2,1)S(1)}, bf16[8,128]{1,0:T(8,128)(2,1)S(1)}, u32[]{:S(2)}, u32[]{:S(2)}) collective-permute-start(bf16[8,128]{1,0:T(8,128)(2,1)S(1)} %get-tuple-element.64), channel_id=1, source_target_pairs={{0,6},{2,4},{4,2},{6,0},{8,14},{10,12},{12,10},{14,8},{1,7},{3,5},... | collective-permute-start | bytes 6152 | tf_op jit(solution)/shard_map/ppermute | solution.py:27
  159.9 7.9 %collective-permute-start.17 = (bf16[8,128]{1,0:T(8,128)(2,1)S(1)}, bf16[8,128]{1,0:T(8,128)(2,1)S(1)}, u32[]{:S(2)}, u32[]{:S(2)}) collective-permute-start(bf16[8,128]{1,0:T(8,128)(2,1)S(1)} %get-tuple-element.63), channel_id=1, source_target_pairs={{0,8},{2,10},{4,12},{6,14},{8,0},{10,2},{12,4},{14,6},{1,9},{3,11}... | collective-permute-start | bytes 6152 | tf_op jit(solution)/shard_map/ppermute | solution.py:27
  160.0 7.8 %collective-permute-start.18 = (bf16[8,128]{1,0:T(8,128)(2,1)S(1)}, bf16[8,128]{1,0:T(8,128)(2,1)S(1)}, u32[]{:S(2)}, u32[]{:S(2)}) collective-permute-start(bf16[8,128]{1,0:T(8,128)(2,1)S(1)} %get-tuple-element.62), channel_id=1, source_target_pairs={{0,10},{2,8},{4,14},{6,12},{8,2},{10,0},{12,6},{14,4},{1,11},{3,9}... | collective-permute-start | bytes 6152 | tf_op jit(solution)/shard_map/ppermute | solution.py:27
  165.7 5.4 %collective-permute-start.19 = (bf16[8,128]{1,0:T(8,128)(2,1)S(1)}, bf16[8,128]{1,0:T(8,128)(2,1)S(1)}, u32[]{:S(2)}, u32[]{:S(2)}) collective-permute-start(bf16[8,128]{1,0:T(8,128)(2,1)S(1)} %get-tuple-element.61), channel_id=1, source_target_pairs={{0,12},{2,14},{4,8},{6,10},{8,4},{10,6},{12,0},{14,2},{1,13},{3,15... | collective-permute-start | bytes 6152 | tf_op jit(solution)/shard_map/ppermute | solution.py:27
  165.8 6.3 %collective-permute-start.20 = (bf16[8,128]{1,0:T(8,128)(2,1)S(1)}, bf16[8,128]{1,0:T(8,128)(2,1)S(1)}, u32[]{:S(2)}, u32[]{:S(2)}) collective-permute-start(bf16[8,128]{1,0:T(8,128)(2,1)S(1)} %get-tuple-element.60), channel_id=1, source_target_pairs={{0,14},{2,12},{4,10},{6,8},{8,6},{10,4},{12,2},{14,0},{1,15},{3,13... | collective-permute-start | bytes 6152 | tf_op jit(solution)/shard_map/ppermute | solution.py:27
  182.0 11.7 %all-to-all-start.3 = ((f32[8,8,128]{2,1,0:T(8,128)}), f32[8,8,128]{2,1,0:T(8,128)S(1)}, u32[]{:S(2)}, u32[]{:S(2)}) async-start(f32[8,8,128]{2,1,0:T(8,128)} %bitcast.96), calls=%async_computation.3 | async-start | bytes 65536 | tf_op jit(solution)/shard_map/all_to_all | solution.py:89
  195.1 38.0 %collective-permute-start.21 = (bf16[8,128]{1,0:T(8,128)(2,1)S(1)}, bf16[8,128]{1,0:T(8,128)(2,1)S(1)}, u32[]{:S(2)}, u32[]{:S(2)}) collective-permute-start(bf16[8,128]{1,0:T(8,128)(2,1)S(1)} %get-tuple-element.58), channel_id=1, source_target_pairs={{0,2},{2,0},{4,6},{6,4},{8,10},{10,8},{12,14},{14,12},{1,3},{3,1},... | collective-permute-start | bytes 6152 | tf_op jit(solution)/shard_map/ppermute | solution.py:27
  227.2 6.1 %collective-permute-start.22 = (bf16[8,128]{1,0:T(8,128)(2,1)S(1)}, bf16[8,128]{1,0:T(8,128)(2,1)S(1)}, u32[]{:S(2)}, u32[]{:S(2)}) collective-permute-start(bf16[8,128]{1,0:T(8,128)(2,1)S(1)} %get-tuple-element.57), channel_id=1, source_target_pairs={{0,4},{2,6},{4,0},{6,2},{8,12},{10,14},{12,8},{14,10},{1,5},{3,7},... | collective-permute-start | bytes 6152 | tf_op jit(solution)/shard_map/ppermute | solution.py:27
  227.3 7.9 %collective-permute-start.23 = (bf16[8,128]{1,0:T(8,128)(2,1)S(1)}, bf16[8,128]{1,0:T(8,128)(2,1)S(1)}, u32[]{:S(2)}, u32[]{:S(2)}) collective-permute-start(bf16[8,128]{1,0:T(8,128)(2,1)S(1)} %get-tuple-element.56), channel_id=1, source_target_pairs={{0,6},{2,4},{4,2},{6,0},{8,14},{10,12},{12,10},{14,8},{1,7},{3,5},... | collective-permute-start | bytes 6152 | tf_op jit(solution)/shard_map/ppermute | solution.py:27
  227.3 7.9 %collective-permute-start.24 = (bf16[8,128]{1,0:T(8,128)(2,1)S(1)}, bf16[8,128]{1,0:T(8,128)(2,1)S(1)}, u32[]{:S(2)}, u32[]{:S(2)}) collective-permute-start(bf16[8,128]{1,0:T(8,128)(2,1)S(1)} %get-tuple-element.55), channel_id=1, source_target_pairs={{0,8},{2,10},{4,12},{6,14},{8,0},{10,2},{12,4},{14,6},{1,9},{3,11}... | collective-permute-start | bytes 6152 | tf_op jit(solution)/shard_map/ppermute | solution.py:27
  227.4 7.8 %collective-permute-start.25 = (bf16[8,128]{1,0:T(8,128)(2,1)S(1)}, bf16[8,128]{1,0:T(8,128)(2,1)S(1)}, u32[]{:S(2)}, u32[]{:S(2)}) collective-permute-start(bf16[8,128]{1,0:T(8,128)(2,1)S(1)} %get-tuple-element.54), channel_id=1, source_target_pairs={{0,10},{2,8},{4,14},{6,12},{8,2},{10,0},{12,6},{14,4},{1,11},{3,9}... | collective-permute-start | bytes 6152 | tf_op jit(solution)/shard_map/ppermute | solution.py:27
  233.2 5.4 %collective-permute-start.26 = (bf16[8,128]{1,0:T(8,128)(2,1)S(1)}, bf16[8,128]{1,0:T(8,128)(2,1)S(1)}, u32[]{:S(2)}, u32[]{:S(2)}) collective-permute-start(bf16[8,128]{1,0:T(8,128)(2,1)S(1)} %get-tuple-element.53), channel_id=1, source_target_pairs={{0,12},{2,14},{4,8},{6,10},{8,4},{10,6},{12,0},{14,2},{1,13},{3,15... | collective-permute-start | bytes 6152 | tf_op jit(solution)/shard_map/ppermute | solution.py:27
  233.3 6.3 %collective-permute-start.27 = (bf16[8,128]{1,0:T(8,128)(2,1)S(1)}, bf16[8,128]{1,0:T(8,128)(2,1)S(1)}, u32[]{:S(2)}, u32[]{:S(2)}) collective-permute-start(bf16[8,128]{1,0:T(8,128)(2,1)S(1)} %get-tuple-element.52), channel_id=1, source_target_pairs={{0,14},{2,12},{4,10},{6,8},{8,6},{10,4},{12,2},{14,0},{1,15},{3,13... | collective-permute-start | bytes 6152 | tf_op jit(solution)/shard_map/ppermute | solution.py:27
  249.3 11.7 %all-to-all-start.4 = ((f32[8,8,128]{2,1,0:T(8,128)}), f32[8,8,128]{2,1,0:T(8,128)S(1)}, u32[]{:S(2)}, u32[]{:S(2)}) async-start(f32[8,8,128]{2,1,0:T(8,128)} %bitcast.123), calls=%async_computation.4 | async-start | bytes 65536 | tf_op jit(solution)/shard_map/all_to_all | solution.py:89
  262.5 38.0 %collective-permute-start.28 = (bf16[8,128]{1,0:T(8,128)(2,1)S(1)}, bf16[8,128]{1,0:T(8,128)(2,1)S(1)}, u32[]{:S(2)}, u32[]{:S(2)}) collective-permute-start(bf16[8,128]{1,0:T(8,128)(2,1)S(1)} %get-tuple-element.50), channel_id=1, source_target_pairs={{0,2},{2,0},{4,6},{6,4},{8,10},{10,8},{12,14},{14,12},{1,3},{3,1},... | collective-permute-start | bytes 6152 | tf_op jit(solution)/shard_map/ppermute | solution.py:27
  294.5 6.1 %collective-permute-start.29 = (bf16[8,128]{1,0:T(8,128)(2,1)S(1)}, bf16[8,128]{1,0:T(8,128)(2,1)S(1)}, u32[]{:S(2)}, u32[]{:S(2)}) collective-permute-start(bf16[8,128]{1,0:T(8,128)(2,1)S(1)} %get-tuple-element.49), channel_id=1, source_target_pairs={{0,4},{2,6},{4,0},{6,2},{8,12},{10,14},{12,8},{14,10},{1,5},{3,7},... | collective-permute-start | bytes 6152 | tf_op jit(solution)/shard_map/ppermute | solution.py:27
  294.6 7.9 %collective-permute-start.30 = (bf16[8,128]{1,0:T(8,128)(2,1)S(1)}, bf16[8,128]{1,0:T(8,128)(2,1)S(1)}, u32[]{:S(2)}, u32[]{:S(2)}) collective-permute-start(bf16[8,128]{1,0:T(8,128)(2,1)S(1)} %get-tuple-element.48), channel_id=1, source_target_pairs={{0,6},{2,4},{4,2},{6,0},{8,14},{10,12},{12,10},{14,8},{1,7},{3,5},... | collective-permute-start | bytes 6152 | tf_op jit(solution)/shard_map/ppermute | solution.py:27
  294.7 7.9 %collective-permute-start.31 = (bf16[8,128]{1,0:T(8,128)(2,1)S(1)}, bf16[8,128]{1,0:T(8,128)(2,1)S(1)}, u32[]{:S(2)}, u32[]{:S(2)}) collective-permute-start(bf16[8,128]{1,0:T(8,128)(2,1)S(1)} %get-tuple-element.47), channel_id=1, source_target_pairs={{0,8},{2,10},{4,12},{6,14},{8,0},{10,2},{12,4},{14,6},{1,9},{3,11}... | collective-permute-start | bytes 6152 | tf_op jit(solution)/shard_map/ppermute | solution.py:27
  294.8 7.8 %collective-permute-start.32 = (bf16[8,128]{1,0:T(8,128)(2,1)S(1)}, bf16[8,128]{1,0:T(8,128)(2,1)S(1)}, u32[]{:S(2)}, u32[]{:S(2)}) collective-permute-start(bf16[8,128]{1,0:T(8,128)(2,1)S(1)} %get-tuple-element.46), channel_id=1, source_target_pairs={{0,10},{2,8},{4,14},{6,12},{8,2},{10,0},{12,6},{14,4},{1,11},{3,9}... | collective-permute-start | bytes 6152 | tf_op jit(solution)/shard_map/ppermute | solution.py:27
  300.5 5.4 %collective-permute-start.33 = (bf16[8,128]{1,0:T(8,128)(2,1)S(1)}, bf16[8,128]{1,0:T(8,128)(2,1)S(1)}, u32[]{:S(2)}, u32[]{:S(2)}) collective-permute-start(bf16[8,128]{1,0:T(8,128)(2,1)S(1)} %get-tuple-element.45), channel_id=1, source_target_pairs={{0,12},{2,14},{4,8},{6,10},{8,4},{10,6},{12,0},{14,2},{1,13},{3,15... | collective-permute-start | bytes 6152 | tf_op jit(solution)/shard_map/ppermute | solution.py:27
  300.6 6.3 %collective-permute-start.34 = (bf16[8,128]{1,0:T(8,128)(2,1)S(1)}, bf16[8,128]{1,0:T(8,128)(2,1)S(1)}, u32[]{:S(2)}, u32[]{:S(2)}) collective-permute-start(bf16[8,128]{1,0:T(8,128)(2,1)S(1)} %get-tuple-element.44), channel_id=1, source_target_pairs={{0,14},{2,12},{4,10},{6,8},{8,6},{10,4},{12,2},{14,0},{1,15},{3,13... | collective-permute-start | bytes 6152 | tf_op jit(solution)/shard_map/ppermute | solution.py:27
  316.7 11.7 %all-to-all-start.5 = ((f32[8,8,128]{2,1,0:T(8,128)}), f32[8,8,128]{2,1,0:T(8,128)S(1)}, u32[]{:S(2)}, u32[]{:S(2)}) async-start(f32[8,8,128]{2,1,0:T(8,128)} %bitcast.150), calls=%async_computation.5 | async-start | bytes 65536 | tf_op jit(solution)/shard_map/all_to_all | solution.py:89
  329.8 38.7 %collective-permute-start.35 = (bf16[8,128]{1,0:T(8,128)(2,1)S(1)}, bf16[8,128]{1,0:T(8,128)(2,1)S(1)}, u32[]{:S(2)}, u32[]{:S(2)}) collective-permute-start(bf16[8,128]{1,0:T(8,128)(2,1)S(1)} %get-tuple-element.42), channel_id=1, source_target_pairs={{0,2},{2,0},{4,6},{6,4},{8,10},{10,8},{12,14},{14,12},{1,3},{3,1},... | collective-permute-start | bytes 6152 | tf_op jit(solution)/shard_map/ppermute | solution.py:27
  362.5 6.1 %collective-permute-start.36 = (bf16[8,128]{1,0:T(8,128)(2,1)S(1)}, bf16[8,128]{1,0:T(8,128)(2,1)S(1)}, u32[]{:S(2)}, u32[]{:S(2)}) collective-permute-start(bf16[8,128]{1,0:T(8,128)(2,1)S(1)} %get-tuple-element.41), channel_id=1, source_target_pairs={{0,4},{2,6},{4,0},{6,2},{8,12},{10,14},{12,8},{14,10},{1,5},{3,7},... | collective-permute-start | bytes 6152 | tf_op jit(solution)/shard_map/ppermute | solution.py:27
  362.6 7.9 %collective-permute-start.37 = (bf16[8,128]{1,0:T(8,128)(2,1)S(1)}, bf16[8,128]{1,0:T(8,128)(2,1)S(1)}, u32[]{:S(2)}, u32[]{:S(2)}) collective-permute-start(bf16[8,128]{1,0:T(8,128)(2,1)S(1)} %get-tuple-element.40), channel_id=1, source_target_pairs={{0,6},{2,4},{4,2},{6,0},{8,14},{10,12},{12,10},{14,8},{1,7},{3,5},... | collective-permute-start | bytes 6152 | tf_op jit(solution)/shard_map/ppermute | solution.py:27
  362.7 7.9 %collective-permute-start.38 = (bf16[8,128]{1,0:T(8,128)(2,1)S(1)}, bf16[8,128]{1,0:T(8,128)(2,1)S(1)}, u32[]{:S(2)}, u32[]{:S(2)}) collective-permute-start(bf16[8,128]{1,0:T(8,128)(2,1)S(1)} %get-tuple-element.39), channel_id=1, source_target_pairs={{0,8},{2,10},{4,12},{6,14},{8,0},{10,2},{12,4},{14,6},{1,9},{3,11}... | collective-permute-start | bytes 6152 | tf_op jit(solution)/shard_map/ppermute | solution.py:27
  362.8 7.8 %collective-permute-start.39 = (bf16[8,128]{1,0:T(8,128)(2,1)S(1)}, bf16[8,128]{1,0:T(8,128)(2,1)S(1)}, u32[]{:S(2)}, u32[]{:S(2)}) collective-permute-start(bf16[8,128]{1,0:T(8,128)(2,1)S(1)} %get-tuple-element.38), channel_id=1, source_target_pairs={{0,10},{2,8},{4,14},{6,12},{8,2},{10,0},{12,6},{14,4},{1,11},{3,9}... | collective-permute-start | bytes 6152 | tf_op jit(solution)/shard_map/ppermute | solution.py:27
  368.5 5.4 %collective-permute-start.40 = (bf16[8,128]{1,0:T(8,128)(2,1)S(1)}, bf16[8,128]{1,0:T(8,128)(2,1)S(1)}, u32[]{:S(2)}, u32[]{:S(2)}) collective-permute-start(bf16[8,128]{1,0:T(8,128)(2,1)S(1)} %get-tuple-element.37), channel_id=1, source_target_pairs={{0,12},{2,14},{4,8},{6,10},{8,4},{10,6},{12,0},{14,2},{1,13},{3,15... | collective-permute-start | bytes 6152 | tf_op jit(solution)/shard_map/ppermute | solution.py:27
  368.6 6.3 %collective-permute-start.41 = (bf16[8,128]{1,0:T(8,128)(2,1)S(1)}, bf16[8,128]{1,0:T(8,128)(2,1)S(1)}, u32[]{:S(2)}, u32[]{:S(2)}) collective-permute-start(bf16[8,128]{1,0:T(8,128)(2,1)S(1)} %get-tuple-element.36), channel_id=1, source_target_pairs={{0,14},{2,12},{4,10},{6,8},{8,6},{10,4},{12,2},{14,0},{1,15},{3,13... | collective-permute-start | bytes 6152 | tf_op jit(solution)/shard_map/ppermute | solution.py:27
  384.7 11.7 %all-to-all-start.7 = ((f32[8,8,128]{2,1,0:T(8,128)}), f32[8,8,128]{2,1,0:T(8,128)S(1)}, u32[]{:S(2)}, u32[]{:S(2)}) async-start(f32[8,8,128]{2,1,0:T(8,128)} %bitcast.183), calls=%async_computation.7 | async-start | bytes 65536 | tf_op jit(solution)/shard_map/all_to_all | solution.py:89
  396.4 10.3 %all-to-all-start.6 = ((f32[8,8,128]{2,1,0:T(8,128)}), f32[8,8,128]{2,1,0:T(8,128)S(1)}, u32[]{:S(2)}, u32[]{:S(2)}) async-start(f32[8,8,128]{2,1,0:T(8,128)} %bitcast.177), calls=%async_computation.6 | async-start | bytes 65536 | tf_op jit(solution)/shard_map/all_to_all | solution.py:89
